TPU v7x, 512 devices: a whole 4x4x16 slice. The times are simulated.
512 devices in a mesh: dp: 16 (over x, z_lo), tensor: 32 (over z_hi, y, core).
Axes of the slice: x: 4, y: 4, z: 16 (z_hi: 4, z_lo: 4; z = z_hi * 4 + z_lo), core: 2. Of those that a mesh axis runs over, the one named last changes fastest.
Arguments:
- layer_input: bfloat16 [16, 192, 4096], P('dp', None, 'tensor'), may hold values from -15 to 15
- frame_mask: int32 [16, 192], P('dp'), may hold values 0 or 1
- w_qkv: bfloat16 [3, 4096, 4096], P(None, None, 'tensor'), may hold values from -0.09375 to 0.09375
- w_out: bfloat16 [4096, 4096], P('tensor'), may hold values from -0.5 to 0.5
- w_in: bfloat16 [4096, 1024], P('tensor'), may hold values from -0.09375 to 0.09375
- step_embed: bfloat16 [17, 1024], replicated, may hold values from -6 to 6
- depth_gain: bfloat16 [1024], replicated, may hold values from 0.5 to 1.5
- cotangent: bfloat16 [16, 192, 17, 1024], P('dp', 'tensor'), may hold values from -6 to 6
Outputs:
- grad_x: bfloat16 [16, 192, 4096], P('dp', None, 'tensor')
- grad_w_in: bfloat16 [4096, 1024], P('tensor')
- grad_step_embed: float32 [17, 1024], replicated
- grad_gain: float32 [1024], replicated
All inputs are finite; a program needn't handle non-finite values. No bound on the sum of `frame_mask` on one device may be relied on, other than what follows from the above.
Results may differ from a plain program's by a relative error of at most 0.03.
Values may be sent and summed in bfloat16 or wider, within the bound.
A program may use at most 64 MiB of HBM per device.

v0:
```python
import jax
import jax.numpy as jnp
from jax import lax
from jax.sharding import PartitionSpec as P


def permitted(mask):
    length = mask.shape[0]
    rows = jnp.arange(length)[:, None]
    cols = jnp.arange(length)[None, :]
    return (cols <= rows) & ((mask[None, :] == 1) | (cols == rows))


def attend(query, key_rows, value, allowed, scale):
    scores = jnp.dot(query, key_rows.T, preferred_element_type=jnp.float32) * scale
    scores = jnp.where(allowed, scores, -1e30)
    probs = jax.nn.softmax(scores, axis=-1)
    rounded = probs.astype(jnp.bfloat16)
    heads = jnp.dot(rounded, value, preferred_element_type=jnp.float32).astype(jnp.bfloat16)
    return (heads, probs, rounded)


def attend_back(grad_heads, query, key_rows, value, probs, rounded, scale):
    grad_probs = jnp.dot(grad_heads, value.T, preferred_element_type=jnp.float32)
    grad_scores = probs * (grad_probs - jnp.sum(probs * grad_probs, axis=-1, keepdims=True)) * scale
    grad_scores = grad_scores.astype(jnp.bfloat16)
    grad_value = jnp.dot(rounded.T, grad_heads, preferred_element_type=jnp.float32).astype(
        jnp.bfloat16
    )
    grad_query = jnp.dot(grad_scores, key_rows, preferred_element_type=jnp.float32).astype(
        jnp.bfloat16
    )
    grad_key = jnp.dot(grad_scores.T, query, preferred_element_type=jnp.float32).astype(
        jnp.bfloat16
    )
    return (grad_query, grad_key, grad_value)


def norm_back(proj, step_embed, depth_gain, cotangent):
    inner = proj[:, None, :] + step_embed.astype(jnp.float32)[None]
    inverse = lax.rsqrt(jnp.mean(inner * inner, axis=-1, keepdims=True) + 1e-06)
    arriving = cotangent.astype(jnp.float32)
    grad_gain = jnp.sum(arriving * inner * inverse, axis=(0, 1))
    scaled = arriving * depth_gain.astype(jnp.float32)
    grad_inner = inverse * scaled - inverse**3 * inner * jnp.mean(
        inner * scaled, axis=-1, keepdims=True
    )
    return (grad_inner, grad_gain)


def shards(layer_input, frame_mask, w_qkv, w_out, w_in, step_embed, depth_gain, cotangent):
    local_rows = layer_input[0]
    length = local_rows.shape[0]
    head_size = w_qkv.shape[2]
    scale = head_size ** (-0.5)
    allowed = permitted(frame_mask[0])
    projected = jnp.einsum(
        "lc,tch->tlh",
        lax.all_gather(layer_input, "tensor", axis=2, tiled=True)[0],
        w_qkv,
        preferred_element_type=jnp.float32,
    ).astype(jnp.bfloat16)
    query, key_rows, value = (projected[0], projected[1], projected[2])
    heads, probs, rounded = attend(query, key_rows, value, allowed, scale)
    out_cols = lax.all_to_all(w_out, "tensor", split_axis=1, concat_axis=0, tiled=True)
    piece = lax.all_gather(heads, "tensor", axis=1, tiled=True)
    count = piece.shape[1] // head_size
    per_head = jnp.einsum(
        "lnh,nhc->nlc",
        piece.reshape(length, count, head_size),
        out_cols.reshape(count, head_size, out_cols.shape[1]),
        preferred_element_type=jnp.float32,
    )
    kept = lax.optimization_barrier(per_head.astype(jnp.bfloat16)).astype(jnp.float32)
    summed = jnp.sum(kept, axis=0)
    hidden = (local_rows.astype(jnp.float32) + summed).astype(jnp.bfloat16)
    proj = lax.psum_scatter(
        jnp.dot(hidden, w_in, preferred_element_type=jnp.float32).astype(jnp.bfloat16),
        "tensor",
        scatter_dimension=0,
        tiled=True,
    ).astype(jnp.float32)
    grad_inner, grad_gain = norm_back(proj, step_embed, depth_gain, cotangent[0])
    grad_step = jnp.sum(grad_inner, axis=0)
    grad_proj = jnp.sum(grad_inner, axis=1).astype(jnp.bfloat16)
    all_grads = lax.all_gather(grad_proj, "tensor", axis=0, tiled=True)
    grad_in = jnp.einsum("lc,ld->cd", hidden, all_grads, preferred_element_type=jnp.float32)
    grad_hidden = jnp.einsum(
        "ld,cd->lc", all_grads, w_in, preferred_element_type=jnp.float32
    ).astype(jnp.bfloat16)
    grad_heads = jnp.einsum(
        "lc,hc->lh",
        lax.all_gather(grad_hidden, "tensor", axis=1, tiled=True),
        w_out,
        preferred_element_type=jnp.float32,
    ).astype(jnp.bfloat16)
    grad_query, grad_key, grad_value = attend_back(
        grad_heads, query, key_rows, value, probs, rounded, scale
    )
    stacked = jnp.stack((grad_query, grad_key, grad_value))
    input_term = jnp.einsum("tlh,tch->lc", stacked, w_qkv, preferred_element_type=jnp.float32)
    input_sum = lax.psum_scatter(
        input_term.astype(jnp.bfloat16), "tensor", scatter_dimension=1, tiled=True
    ).astype(jnp.float32)
    grad_x = (grad_hidden.astype(jnp.float32) + input_sum).astype(jnp.bfloat16)[None]
    grad_in_sum = lax.psum(grad_in.astype(jnp.bfloat16), "dp")
    step_sum, gain_sum = lax.psum((grad_step, grad_gain), ("dp", "tensor"))
    return (grad_x, grad_in_sum, step_sum, gain_sum)


def solution(mesh):
    return jax.shard_map(
        shards,
        mesh=mesh,
        in_specs=(
            P("dp", None, "tensor"),
            P("dp", None),
            P(None, None, "tensor"),
            P("tensor", None),
            P("tensor", None),
            P(),
            P(),
            P("dp", "tensor", None, None),
        ),
        out_specs=(P("dp", None, "tensor"), P("tensor", None), P(), P()),
        check_vma=False,
    )
```

profile of v0, /device:TPU:24, one launch (start us, length us, event | category | flops | bytes accessed | tf_op | source)
XLA Modules:
  0.0 1202.8 jit_solution(15451372445256188298)
XLA Ops:
  7.2 0.7 all-gather.5.cloned.1.call-update
  7.9 2.5 copy.16
  10.4 2.3 copy.17
  12.6 18.2 %all-to-all-start = ((bf16[128,32,128]{2,0,1:T(8,128)(2,1)}), bf16[128,32,128]{2,0,1:T(8,128)(2,1)}, u32[]{:S(2)}, u32[]{:S(2)}) async-start(bf16[128,32,128]{2,0,1:T(8,128)(2,1)} %copy.17), calls=%async_computation | async-start | bytes 2097152 | tf_op jit(solution)/shard_map/all_to_all | solution.py:65
  30.9 91.5 %all-gather.5.cloned.1.call-done = bf16[1,192,4096]{2,1,0:T(8,128)(2,1)} async-done(((bf16[1,192,128]{2,1,0:T(8,128)(2,1)}), bf16[1,192,4096]{2,1,0:T(8,128)(2,1)}) %all-gather.5.cloned.1.call-update) | async-done | bytes 1572880 | tf_op jit(solution)/shard_map/all_gather | solution.py:59
  122.4 2.4 fusion.10
  124.8 0.2 fusion.45
  125.1 0.3 copy-done.6
  125.4 0.3 copy-done.3
  125.7 0.6 copy-done.10
  126.3 0.8 convolution_convert_fusion.7
  127.2 71.5 %all-gather.7.cloned.1.call-done = bf16[192,4096]{1,0:T(8,128)(2,1)} async-done(((bf16[192,128]{1,0:T(8,128)(2,1)}), bf16[192,4096]{1,0:T(8,128)(2,1)}) %all-gather.7.cloned.1.call-update) | async-done | bytes 1572880 | tf_op jit(solution)/shard_map/all_gather | solution.py:66
  198.7 2.3 convolution_convert_fusion
  201.2 0.6 copy-done.2
  201.9 0.2 convolution_convert_fusion.1
  202.2 81.6 %fusion = bf16[8,1024]{1,0:T(8,128)(2,1)S(1)} fusion(bf16[192,1024]{1,0:T(8,128)(2,1)S(1)} %convolution_convert_fusion.1), kind=kCustom, calls=%all-reduce-scatter | all-reduce-scatter fusion | flops 262145 | bytes 411648
  283.8 7.8 collective-permute-start
  291.6 10.1 collective-permute-start.1
  301.8 4.2 collective-permute-start.7
  306.0 1.9 collective-permute-start.2
  307.9 7.0 collective-permute-start.3
  314.9 1.9 collective-permute-start.4
  316.9 2.8 collective-permute-start.5
  319.7 1.8 collective-permute-start.6
  321.5 0.8 convert_element_type.92
  322.3 0.7 convert_element_type.95
  323.0 1.3 dynamic-slice.4
  325.0 1.0 concatenate
  326.0 1.2 fusion.19
  327.2 2.0 fusion.24
  329.2 50.8 %all-gather = bf16[32,6,1024]{2,1,0:T(8,128)(2,1)} all-gather(bf16[1,6,1024]{2,1,0:T(8,128)(2,1)S(1)} %bitcast.84), channel_id=1, replica_groups=mesh['dp'=16,'tensor'=32] {'tensor'}, dimensions={0}, use_global_device_ids=true | all-gather | bytes 405504 | tf_op jit(solution)/shard_map/all_gather | solution.py:86
  380.0 1.2 reshape.48
  381.2 1.8 convolution_convert_fusion.6
  383.2 75.5 %all-gather.9.cloned.1.call-done = bf16[192,4096]{1,0:T(8,128)(2,1)} async-done(((bf16[192,128]{1,0:T(8,128)(2,1)}), bf16[192,4096]{1,0:T(8,128)(2,1)}) %all-gather.9.cloned.1.call-update) | async-done | bytes 1572880 | tf_op jit(solution)/shard_map/all_gather | solution.py:93
  458.6 2.3 convolution_convert_fusion.8
  461.0 0.2 multiply_reduce_fusion
  461.8 2.4 fusion.1
  464.2 3.8 copy.19
  468.1 0.5 all-reduce.7.cloned.1.call-update
  468.7 1.9 convolution_convert_fusion.2
  470.6 106.7 %psum.23 = f32[1024]{0:T(1024)} all-reduce(f32[1024]{0:T(1024)S(1)} %get-tuple-element.6), channel_id=1, replica_groups=mesh['dp'=16,'tensor'=32] {'dp','tensor'}, use_global_device_ids=true, to_apply=%region_13.14 | all-reduce | flops 1024 | bytes 8192 | tf_op jit(solution)/shard_map/psum | solution.py:107
  577.3 5.8 reduce-scatter.6.cloned.1.call-done
  583.1 0.9 copy.20
  584.0 1.4 fusion.36
  585.5 440.8 %all-reduce.7.cloned.1.call-done = f32[17,1024]{1,0:T(8,128)} async-done(((f32[17,1024]{1,0:T(8,128)}), f32[17,1024]{1,0:T(8,128)}) %all-reduce.7.cloned.1.call-update) | async-done | bytes 69648 | tf_op jit(solution)/shard_map/psum | solution.py:107
  1026.3 166.4 %all-reduce.5.cloned.1.call-done = bf16[128,1024]{1,0:T(8,128)(2,1)} async-done(((bf16[128,1024]{1,0:T(8,128)(2,1)}), bf16[128,1024]{1,0:T(8,128)(2,1)}) %all-reduce.5.cloned.1.call-update) | async-done | bytes 262160 | tf_op jit(solution)/shard_map/psum | solution.py:106
  1192.7 1.7 copy.28
  1194.4 1.5 copy.29
  (51 shorter events, 1.4 us)
Async XLA Ops:
  7.2 115.2 %copy-start = (bf16[3,4096,128]{2,1,0:T(8,128)(2,1)S(1)}, bf16[3,4096,128]{2,1,0:T(8,128)(2,1)}, u32[]{:S(2)}) copy-start(bf16[3,4096,128]{2,1,0:T(8,128)(2,1)} %param.10) | copy-start | bytes 9437188
  7.2 115.2 %all-gather.5.cloned.1.call-start = ((), (), s32[]{:S(2)}) async-start(), calls=%async_computation.2 | async-start | bytes 1622016 | tf_op jit(solution)/shard_map/all_gather | solution.py:59
  10.4 20.5 %copy-start.12 = (s32[1,192]{1,0:T(1,128)S(1)}, s32[1,192]{1,0:T(1,128)}, u32[]{:S(2)}) copy-start(s32[1,192]{1,0:T(1,128)} %param.9) | copy-start | bytes 2308
  12.6 114.5 %all-to-all-start = ((bf16[128,32,128]{2,0,1:T(8,128)(2,1)}), bf16[128,32,128]{2,0,1:T(8,128)(2,1)}, u32[]{:S(2)}, u32[]{:S(2)}) async-start(bf16[128,32,128]{2,0,1:T(8,128)(2,1)} %copy.17), calls=%async_computation | async-start | bytes 2097152 | tf_op jit(solution)/shard_map/all_to_all | solution.py:65
  30.8 167.9 %all-gather.7.cloned.1.call-start = ((), (), s32[]{:S(2)}) async-start(), calls=%async_computation.3 | async-start | bytes 1622016 | tf_op jit(solution)/shard_map/all_gather | solution.py:66
  124.8 0.7 copy-start.6
  125.0 0.7 copy-start.3
  125.0 0.7 copy-start.8
  125.7 0.6 copy-start.10
  127.1 331.5 %all-gather.9.cloned.1.call-start = ((), (), s32[]{:S(2)}) async-start(), calls=%async_computation.4 | async-start | bytes 1622016 | tf_op jit(solution)/shard_map/all_gather | solution.py:93
  201.0 1.0 copy-start.1
  201.0 0.9 copy-start.5
  201.2 0.6 copy-start.2
  283.8 33.0 %collective-permute-start = (bf16[8,1024]{1,0:T(8,128)(2,1)S(1)}, bf16[8,1024]{1,0:T(8,128)(2,1)S(1)}, u32[]{:S(2)}, u32[]{:S(2)}) collective-permute-start(bf16[8,1024]{1,0:T(8,128)(2,1)S(1)} %fusion), channel_id=1, source_target_pairs={{0,1},{1,2},{2,3},{3,4},{4,5},{5,6},{6,7},{7,8},{8,9},{9,10},{10,1... | collective-permute-start | bytes 49160
  291.6 28.1 %collective-permute-start.1 = (bf16[8,1024]{1,0:T(8,128)(2,1)S(1)}, bf16[8,1024]{1,0:T(8,128)(2,1)S(1)}, u32[]{:S(2)}, u32[]{:S(2)}) collective-permute-start(bf16[8,1024]{1,0:T(8,128)(2,1)S(1)} %fusion), channel_id=1, source_target_pairs={{0,2},{1,3},{2,4},{3,5},{4,6},{5,7},{6,8},{7,9},{8,10},{9,11},{10,... | collective-permute-start | bytes 49160
  301.8 13.1 %collective-permute-start.7 = (bf16[6,1024]{1,0:T(8,128)(2,1)S(1)}, bf16[6,1024]{1,0:T(8,128)(2,1)S(1)}, u32[]{:S(2)}, u32[]{:S(2)}) collective-permute-start(bf16[6,1024]{1,0:T(8,128)(2,1)S(1)} %slice.15), channel_id=1, source_target_pairs={{0,8},{1,9},{2,10},{3,11},{4,12},{5,13},{6,14},{7,15},{8,16},{9,17... | collective-permute-start | bytes 36872
  306.0 18.9 %collective-permute-start.2 = (bf16[8,1024]{1,0:T(8,128)(2,1)S(1)}, bf16[8,1024]{1,0:T(8,128)(2,1)S(1)}, u32[]{:S(2)}, u32[]{:S(2)}) collective-permute-start(bf16[8,1024]{1,0:T(8,128)(2,1)S(1)} %fusion), channel_id=1, source_target_pairs={{0,3},{1,4},{2,5},{3,6},{4,7},{5,8},{6,9},{7,10},{8,11},{9,12},{10... | collective-permute-start | bytes 49160
  307.9 17.0 %collective-permute-start.3 = (bf16[8,1024]{1,0:T(8,128)(2,1)S(1)}, bf16[8,1024]{1,0:T(8,128)(2,1)S(1)}, u32[]{:S(2)}, u32[]{:S(2)}) collective-permute-start(bf16[8,1024]{1,0:T(8,128)(2,1)S(1)} %fusion), channel_id=1, source_target_pairs={{0,4},{1,5},{2,6},{3,7},{4,8},{5,9},{6,10},{7,11},{8,12},{9,13},{1... | collective-permute-start | bytes 49160
  314.9 10.0 collective-permute-start.4
  316.9 8.1 collective-permute-start.5
  319.7 5.3 collective-permute-start.6
  381.2 79.7 %copy-start.9 = (f32[192]{0:T(256)S(1)}, f32[192]{0:T(256)}, u32[]{:S(2)}) copy-start(f32[192]{0:T(256)} %copy-done.8) | copy-start | bytes 2308
  381.2 79.7 %copy-start.11 = (f32[192]{0:T(256)S(1)}, f32[192]{0:T(256)}, u32[]{:S(2)}) copy-start(f32[192]{0:T(256)} %copy-done.10) | copy-start | bytes 2308
  383.1 200.0 %reduce-scatter.6.cloned.1.call-start = ((), (), s32[]{:S(2)}) async-start(), calls=%async_computation.7 | async-start | bytes 2162688
  458.6 2.3 copy-start.4
  458.6 2.4 copy-start.7
  468.1 558.2 %all-reduce.7.cloned.1.call-start = ((), (), s32[]{:S(2)}) async-start(), calls=%async_computation.6 | async-start | bytes 196608 | tf_op jit(solution)/shard_map/psum | solution.py:107
  468.7 724.1 %all-reduce.5.cloned.1.call-start = ((), (), s32[]{:S(2)}) async-start(), calls=%async_computation.5 | async-start | bytes 524288 | tf_op jit(solution)/shard_map/psum | solution.py:106
Sparse Core Ops, SparseCore 0:
  11.1 111.2 all-gather.4
  127.3 71.4 all-gather.6
  383.2 75.3 all-gather.8
  468.2 114.8 reduce-scatter.5
  589.0 437.3 all-reduce.6
  1029.9 162.7 all-reduce.4
where the time goes:
time: 1200 us
  waiting for transfers between devices  853 us (71%)
  blocking collectives  239 us (20%)
  starting transfers between devices  56 us (5%)
  local copies, waits for them, and re-layouts  18 us (2%)
  matrix products  15.1 us (1%)
  between operations  15.1 us (1%)
    psum x1, waiting for transfers between devices, shards(): step_sum, gain_sum = lax.psum((grad_step, grad_gain), ('dp', 'tensor'))  441 us
    psum x1, waiting for transfers between devices, shards(): grad_in_sum = lax.psum(grad_in.astype(jnp.bfloat16), 'dp')  166 us
    psum x1, blocking collectives, shards(): step_sum, gain_sum = lax.psum((grad_step, grad_gain), ('dp', 'tensor'))  107 us
    all_gather x1, waiting for transfers between devices, shards(): lax.all_gather(layer_input, 'tensor', axis=2, tiled=True)[0]  91.5 us
    unnamed x1, blocking collectives  81.6 us
    all_gather x1, waiting for transfers between devices, shards(): lax.all_gather(grad_hidden, 'tensor', axis=1, tiled=True)  75.5 us
    all_gather x1, waiting for transfers between devices, shards(): piece = lax.all_gather(heads, 'tensor', axis=1, tiled=True)  71.5 us
    all_gather x1, blocking collectives, shards(): all_grads = lax.all_gather(grad_proj, 'tensor', axis=0, tiled=True)  50.8 us
  transfers between devices with their start and end apart: 15, of which 6 were waited for; matrix products, arithmetic and copies ran while one was open for 1% of the time, Pallas kernels for 0%

commit v1 on v0

v1 whole, which is shorter than its diff:
```python
import functools

import jax
import jax.numpy as jnp
from jax import lax
from jax.experimental import pallas as pl
from jax.experimental.pallas import tpu as pltpu
from jax.sharding import PartitionSpec as P

MESH = pl.DeviceIdType.MESH
F32 = jnp.float32
BF16 = jnp.bfloat16
L, HD, DD, STEPS, FR = 192, 128, 1024, 17, 6
HALF = L // 2
LO, HI = pl.ds(0, HALF), pl.ds(HALF, HALF)
ROWS = FR * (DD // HD)
PIECE = 64
N_SEM = 200


def nt(a, b):
    return lax.dot_general(a, b, (((1,), (1,)), ((), ())), preferred_element_type=F32)


def nn(a, b):
    return lax.dot_general(a, b, (((1,), (0,)), ((), ())), preferred_element_type=F32)


def tn(a, b):
    return lax.dot_general(a, b, (((0,), (0,)), ((), ())), preferred_element_type=F32)


def around(v):
    return (v + 1) % 4, (v + 3) % 4, (v + 2) % 4


class Net:
    def __init__(self, send_sems, recv_sems):
        self.send_sems, self.recv_sems = send_sems, recv_sems
        self.count = 0
        self.open = []
        dp, t = lax.axis_index("dp"), lax.axis_index("tensor")
        self.dp, self.t = dp, t
        self.x, self.zl = dp // 4, dp % 4
        self.z, self.y, self.c = t // 8, (t // 2) % 4, t % 2

    def go(self, z=0, y=0, c=0, x=0, zl=0):
        dp, t = self.dp, self.t
        if x or zl:
            dp = ((self.x + x) % 4) * 4 + (self.zl + zl) % 4
        if z or y or c:
            cc = (self.c + c) % 2
            t = ((self.z + z) % 4) * 8 + ((self.y + y) % 4) * 2 + cc
        return (dp, t)

    def peers(self):
        found = [self.go(c=1)]
        for d in (1, 2, 3):
            found += [self.go(y=d), self.go(z=d), self.go(x=d), self.go(zl=d)]
        return found

    def make(self, src, dst, peer):
        i = self.count
        self.count += 1
        return pltpu.make_async_remote_copy(
            src_ref=src,
            dst_ref=dst,
            send_sem=self.send_sems.at[i],
            recv_sem=self.recv_sems.at[i],
            device_id=peer,
            device_id_type=MESH,
        )

    def send(self, src, dst, peer):
        copy = self.make(src, dst, peer)
        copy.start()
        self.open.append(copy)
        return copy

    def drain(self):
        for copy in self.open:
            copy.wait_send()
        self.open = []


class Gather:
    def __init__(self, net, g):
        self.net, self.g = net, g
        self.planes = (net.z, around(net.z)[1], around(net.z)[0], around(net.z)[2])
        self.along, self.forward, self.across = {}, {}, {}
        self.to_yp, self.to_ym, self.to_c = net.go(y=1), net.go(y=3), net.go(c=1)

    def whole(self, zz, yy, peer):
        at = self.g.at[zz, yy, self.net.c]
        return self.net.send(at, at, peer)

    def part(self, zz, yy, rows, peer):
        at = self.g.at[zz, yy, self.net.c, rows]
        return self.net.send(at, at, peer)

    def begin(self):
        z, y = self.net.z, self.net.y
        to_zp, to_zm = self.net.go(z=1), self.net.go(z=3)
        self.up_lo = self.part(z, y, LO, to_zp)
        self.dn_hi = self.part(z, y, HI, to_zm)
        self.up_hi = self.part(z, y, HI, to_zp)
        self.dn_lo = self.part(z, y, LO, to_zm)
        self.spread(0)

    def along_z(self):
        y = self.net.y
        to_zp, to_zm = self.net.go(z=1), self.net.go(z=3)
        self.up_lo.wait_recv()
        self.on = self.part(self.planes[1], y, LO, to_zp)
        self.dn_hi.wait_recv()
        self.back = self.part(self.planes[2], y, HI, to_zm)
        self.up_hi.wait_recv()
        self.spread(1)
        self.dn_lo.wait_recv()
        self.spread(2)

    def far_z(self):
        self.on.wait_recv()
        self.back.wait_recv()
        self.spread(3)

    def spread(self, i):
        zz, y = self.planes[i], self.net.y
        self.along[i] = (self.whole(zz, y, self.to_yp), self.whole(zz, y, self.to_ym))
        self.across[i] = []
        self.over(i, zz, y)

    def over(self, i, zz, yy):
        if i == 3:
            self.across[i].append(self.whole(zz, yy, self.to_c))

    def turn(self, i):
        zz = self.planes[i]
        yp, ym, _ = around(self.net.y)
        self.along[i][0].wait_recv()
        first = self.part(zz, ym, LO, self.to_yp)
        self.over(i, zz, ym)
        self.along[i][1].wait_recv()
        second = self.part(zz, yp, HI, self.to_ym)
        self.over(i, zz, yp)
        self.forward[i] = (first, second)

    def land(self, i):
        for copy in self.forward[i]:
            copy.wait_recv()
        self.over(i, self.planes[i], around(self.net.y)[2])
        if i < 3:
            at = self.g.at[self.planes[i], pl.ds(0, 4), self.net.c]
            self.across[i].append(self.net.send(at, at, self.to_c))

    def here(self, i):
        for copy in self.across[i]:
            copy.wait_recv()


def scatter_ring(net, p, fill, bufs, done, early=False):
    ya, yb, yup, ydn, q, za, zb, zup, zdn = bufs
    z, y = net.z, net.y
    zp, zm, z2 = around(z)
    yp, ym, y2 = around(y)
    to_zp, to_zm, to_yp, to_ym = net.go(z=1), net.go(z=3), net.go(y=1), net.go(y=3)
    order = (z2, zp, zm, z)

    pairs = (order[:2], order[2:])
    if early:
        for yy in (y2, yp, ym, y):
            for pair in pairs:
                fill(yy, pair)
        yield
    far = []
    for pair in pairs:
        if not early:
            fill(y2, pair)
        for zz in pair:
            far.append(
                (
                    net.send(p.at[zz, y2, LO], ya.at[zz], to_yp),
                    net.send(p.at[zz, y2, HI], yb.at[zz], to_ym),
                )
            )
    yield
    if not early:
        for pair in pairs:
            fill(yp, pair)
            fill(ym, pair)
        yield
    near = []
    for i, zz in enumerate(order):
        far[i][0].wait_recv()
        p[zz, yp, LO] = (p[zz, yp, LO].astype(F32) + ya[zz].astype(F32)).astype(BF16)
        up = net.send(p.at[zz, yp], yup.at[zz], to_yp)
        far[i][1].wait_recv()
        p[zz, ym, HI] = (p[zz, ym, HI].astype(F32) + yb[zz].astype(F32)).astype(BF16)
        near.append((up, net.send(p.at[zz, ym], ydn.at[zz], to_ym)))
    if not early:
        for pair in pairs:
            fill(y, pair)
    yield

    def mine(i):
        near[i][0].wait_recv()
        near[i][1].wait_recv()
        zz = order[i]
        return p[zz, y].astype(F32) + yup[zz].astype(F32) + ydn[zz].astype(F32)

    q[0] = mine(0).astype(BF16)
    a = net.send(q.at[0, LO], za, to_zp)
    b = net.send(q.at[0, HI], zb, to_zm)
    yield
    q[1] = mine(1).astype(BF16)
    q[2] = mine(2).astype(BF16)
    yield
    a.wait_recv()
    q[1, LO] = (q[1, LO].astype(F32) + za[...].astype(F32)).astype(BF16)
    up = net.send(q.at[1], zup, to_zp)
    b.wait_recv()
    q[2, HI] = (q[2, HI].astype(F32) + zb[...].astype(F32)).astype(BF16)
    down = net.send(q.at[2], zdn, to_zm)
    yield
    total = mine(3)
    yield
    up.wait_recv()
    down.wait_recv()
    done(total + zup[...].astype(F32) + zdn[...].astype(F32))


def kernel(
    x_hbm, mask_hbm, step_hbm, gain_hbm, wqkv_hbm, wout_hbm, win_hbm, cot_hbm,
    gx_ref, gw_ref, gs_ref, gg_ref,
    xg, maskv, stepv, gainv, wq, wqp, wo, wop, wi, wit, witp, cot,
    gm, mt, mtp,
    acc, qs, ks, vs, probs_s, hp, p1, hid, pf, p2, pyb, pq, pzb, pr, gpf,
    gpg, gpr, gpn, ghs, p3, gr, rows_s,
    wst, wxb, wsm, wzb, wfin,
    sst, syb, sm1, sxb, szb, slb, scb, sfin,
    *rest,
):
    bufs1, bufs2 = rest[:9], rest[9:18]
    send_sems, recv_sems, local_sems = rest[18:]
    net = Net(send_sems, recv_sems)
    x, zl, z, y, c = net.x, net.zl, net.z, net.y, net.c
    to_c = net.go(c=1)
    scale = HD ** (-0.5)

    barrier = pltpu.get_barrier_semaphore()
    peers = net.peers()
    for peer in peers:
        pl.semaphore_signal(barrier, inc=1, device_id=peer, device_id_type=MESH)
    loads = {}
    for i, (name, src, dst) in enumerate(
        (
            ("w_in", win_hbm, wi),
            ("x", x_hbm, xg.at[z, y, c]),
            ("w_out", wout_hbm, wo),
            ("w_qkv", wqkv_hbm, wq),
            ("mask", mask_hbm, maskv),
            ("step", step_hbm, stepv),
            ("gain", gain_hbm, gainv),
            ("cot", cot_hbm, cot),
        )
    ):
        loads[name] = pltpu.make_async_copy(src, dst, local_sems.at[i])
        loads[name].start()
    loads["w_in"].wait()
    for k in range(8):
        wit[k * HD : (k + 1) * HD, :] = wi[:, k * HD : (k + 1) * HD].T
    gm[z, y, c] = wit[pl.ds(pl.multiple_of(PIECE * net.dp, PIECE), PIECE), :]
    loads["x"].wait()
    pl.semaphore_wait(barrier, len(peers))

    every = pl.ds(0, 4)

    def weight_product():
        sent = [net.send(gm.at[z, y, c], gm.at[z, y, c], net.go(z=d)) for d in (1, 2, 3)]
        yield
        for copy in sent:
            copy.wait_recv()
        sent = [net.send(gm.at[every, y, c], gm.at[every, y, c], net.go(y=d)) for d in (1, 2, 3)]
        yield
        for copy in sent:
            copy.wait_recv()
        other = net.send(gm.at[every, every, c], gm.at[every, every, c], to_c)
        yield
        other.wait_recv()
        loads["w_out"].wait()
        left = jnp.concatenate(
            [gm[i, j, k] for i in range(4) for j in range(4) for k in range(2)], axis=1
        )
        mt[x, zl] = nt(left, wo[...]).astype(BF16)
        sent = [net.send(mt.at[x, zl], mt.at[x, zl], net.go(zl=d)) for d in (1, 2, 3)]
        yield
        for copy in sent:
            copy.wait_recv()
        sent = [net.send(mt.at[x], mt.at[x], net.go(x=d)) for d in (1, 2, 3)]
        last = [net.send(mt.at[x], mtp.at[x], to_c)]
        yield
        for d in (1, 2, 3):
            sent[d - 1].wait_recv()
            spot = (x + 4 - d) % 4
            last.append(net.send(mt.at[spot], mtp.at[spot], to_c))
        yield
        for copy in last:
            copy.wait_recv()

    def plane(i):
        zz = gather.planes[i]
        gather.here(i)
        left = jnp.concatenate([xg[zz, j, k] for j in range(4) for k in range(2)], axis=1)
        right = jnp.concatenate([wq[j, zz].reshape(DD, HD) for j in range(3)], axis=1)
        term = nn(left, right)
        acc[...] = term if i == 0 else acc[...] + term

    product = weight_product()
    next(product)
    gather = Gather(net, xg)
    gather.begin()
    next(product)
    gather.along_z()
    next(product)
    gather.turn(0)
    gather.far_z()
    gather.turn(1)
    gather.turn(2)
    gather.land(0)
    next(product)
    gather.turn(3)
    gather.land(1)
    gather.land(2)
    loads["w_qkv"].wait()
    plane(0)
    next(product)
    plane(1)
    gather.land(3)
    partner_in = net.send(wit, witp, to_c)
    plane(2)
    plane(3)

    spot = net.count
    partner_out = net.make(wop, wop, to_c)
    for i in range(16):
        cols = pl.ds(pl.multiple_of((2 * i + 1 - c) * HD, HD), HD)
        pltpu.make_async_remote_copy(
            src_ref=wout_hbm.at[:, cols],
            dst_ref=wop.at[i],
            send_sem=send_sems.at[spot],
            recv_sem=recv_sems.at[spot],
            device_id=to_c,
            device_id_type=MESH,
        ).start()
    net.open.append(partner_out)
    partner_qkv = []

    def swap_qkv(j):
        partner_qkv.append(net.send(wqkv_hbm.at[j, every, every, 1 - c], wqp.at[j], to_c))

    swap_qkv(0)

    query = acc[:, :HD].astype(BF16)
    key_rows = acc[:, HD : 2 * HD].astype(BF16)
    value = acc[:, 2 * HD :].astype(BF16)
    qs[...] = query
    ks[...] = key_rows
    vs[...] = value
    loads["mask"].wait()
    row = lax.broadcasted_iota(jnp.int32, (L, L), 0)
    col = lax.broadcasted_iota(jnp.int32, (L, L), 1)
    allowed = (col <= row) & ((maskv[...] == 1) | (col == row))
    scores = jnp.where(allowed, nt(query, key_rows) * scale, -1e30)
    next(product)
    raised = jnp.exp(scores - jnp.max(scores, axis=-1, keepdims=True))
    probs = raised / jnp.sum(raised, axis=-1, keepdims=True)
    probs_s[...] = probs
    hp[0] = nn(probs.astype(BF16), value).astype(BF16)
    heads_copy = net.send(hp.at[0], hp.at[1], to_c)
    partner_in.wait_recv()
    next(product, None)
    heads_copy.wait_recv()

    left = jnp.concatenate([hp[0], hp[1], xg[z, y, c], xg[z, y, 1 - c]], axis=1)
    right = jnp.concatenate(
        [mt[...].reshape(DD, HD), mtp[...].reshape(DD, HD), wit[...], witp[...]], axis=1
    )
    term = nt(left, right)
    for k in range(8):
        pf[pl.ds(k, L, stride=8), :] = term[:, k * HD : (k + 1) * HD]
    for i in range(4):
        for j in range(4):
            rows = pl.ds(pl.multiple_of((8 * i + 2 * j + c) * ROWS, 8), ROWS)
            p2[j, i] = pf[rows, :].astype(BF16)
    sent = [net.send(p2.at[(y + d) % 4], pyb.at[d - 1], net.go(y=d)) for d in (1, 2, 3)]
    def fill_out(yy, pair):
        left = jnp.concatenate([hp[0], hp[1]], axis=1)
        right = []
        for zz in pair:
            col0 = pl.multiple_of((zz * 8 + yy * 2 + c) * HD, HD)
            right.append(jnp.concatenate([wo[:, pl.ds(col0, HD)], wop[zz * 4 + yy]], axis=0))
        term = nn(left, jnp.concatenate(right, axis=1)).astype(BF16)
        p1[pair[0], yy] = term[:, :HD]
        p1[pair[1], yy] = term[:, HD:]

    def keep_hidden(summed):
        hid[...] = (xg[z, y, c].astype(F32) + summed).astype(BF16)

    outward = scatter_ring(net, p1, fill_out, bufs1, keep_hidden, early=True)
    partner_out.wait_recv()
    next(outward)
    total = p2[y].astype(F32)
    for d in range(3):
        sent[d].wait_recv()
        total += pyb[d].astype(F32)
    pq[...] = total.astype(BF16)
    sent = [net.send(pq.at[(z + d) % 4], pzb.at[d - 1], net.go(z=d)) for d in (1, 2, 3)]

    next(outward)
    total = pq[z].astype(F32)
    for d in range(3):
        sent[d].wait_recv()
        total += pzb[d].astype(F32)
    pr[...] = total
    swap_qkv(1)

    for name in ("step", "gain", "cot"):
        loads[name].wait()
    gains = gainv[...].astype(F32)[None]
    proj = jnp.concatenate([pr[pl.ds(k, FR, stride=8), :] for k in range(8)], axis=1)
    grad_rows = jnp.zeros((FR, DD), F32)
    gain_rows = jnp.zeros((FR, DD), F32)
    for s in range(STEPS):
        inner = proj + stepv[s : s + 1, :].astype(F32)
        inverse = lax.rsqrt(jnp.mean(inner * inner, axis=-1, keepdims=True) + 1e-06)
        arriving = cot[s].astype(F32)
        gain_rows += arriving * inner * inverse
        scaled = arriving * gains
        mixed = jnp.mean(inner * scaled, axis=-1, keepdims=True)
        grad_inner = inverse * scaled - inverse * inverse * inverse * inner * mixed
        grad_rows += grad_inner
        rows_s[s : s + 1, :] = jnp.sum(grad_inner, axis=0, keepdims=True)
    for k in range(8):
        gpf[pl.ds(k, FR, stride=8), :] = grad_rows[:, k * HD : (k + 1) * HD]
    gpg[z, y, c] = gpf[...].astype(BF16)

    sent = [net.send(gpg.at[z, y, c], gpg.at[z, y, c], net.go(z=d)) for d in (1, 2, 3)]
    rows_s[STEPS : STEPS + 1, :] = jnp.sum(gain_rows, axis=0, keepdims=True)
    for k in range(8):
        cols = slice(k * HD, (k + 1) * HD)
        j, i = k // 2, 2 * (k % 2)
        sst[j, i] = rows_s[:16, cols]
        sst[j, i + 1] = jnp.zeros((16, HD), F32)
        sst[j, i + 1, 0:2] = rows_s[16:18, cols]

    def small_sums():
        sent = [net.send(sst.at[(y + d) % 4], syb.at[d - 1], net.go(y=d)) for d in (1, 2, 3)]
        yield
        total = sst[y]
        for d in range(3):
            sent[d].wait_recv()
            total += syb[d]
        sm1[...] = total
        sent = [net.send(sm1.at[(x + d) % 4], sxb.at[d - 1], net.go(x=d)) for d in (1, 2, 3)]
        yield
        total = sm1[x]
        for d in range(3):
            sent[d].wait_recv()
            total += sxb[d]
        szb[z] = total
        sent = [net.send(szb.at[z], szb.at[z], net.go(z=d)) for d in (1, 2, 3)]
        yield
        for copy in sent:
            copy.wait_recv()
        slb[zl] = szb[0] + szb[1] + szb[2] + szb[3]
        sent = [net.send(slb.at[zl], slb.at[zl], net.go(zl=d)) for d in (1, 2, 3)]
        yield
        for copy in sent:
            copy.wait_recv()
        scb[c] = slb[0] + slb[1] + slb[2] + slb[3]
        other = net.send(scb.at[c], scb.at[c], to_c)
        yield
        other.wait_recv()
        sfin[y, x] = scb[0] + scb[1]
        sent = [net.send(sfin.at[y, x], sfin.at[y, x], net.go(x=d)) for d in (1, 2, 3)]
        yield
        for copy in sent:
            copy.wait_recv()
        sent = [net.send(sfin.at[y], sfin.at[y], net.go(y=d)) for d in (1, 2, 3)]
        yield
        for copy in sent:
            copy.wait_recv()
        for k in range(8):
            cols = slice(k * HD, (k + 1) * HD)
            j, i = k // 2, 2 * (k % 2)
            gs_ref[0:16, cols] = sfin[j, i]
            gs_ref[16:17, cols] = sfin[j, i + 1, 0:1]
            gg_ref[0:1, cols] = sfin[j, i + 1, 1:2]

    def weight_sums():
        grads = tn(hid[...], gpn[...]).astype(BF16)
        for k in range(8):
            cols = slice(k * HD, (k + 1) * HD)
            wst[2 * k] = grads[:64, cols]
            wst[2 * k + 1] = grads[64:, cols]
        sent = []
        for d in (1, 2, 3):
            rows = pl.ds(4 * ((x + d) % 4), 4)
            sent.append(net.send(wst.at[rows], wxb.at[d - 1], net.go(x=d)))
        yield
        total = wst[pl.ds(4 * x, 4)].astype(F32)
        for d in range(3):
            sent[d].wait_recv()
            total += wxb[d].astype(F32)
        wsm[...] = total.astype(BF16)
        sent = [net.send(wsm.at[(zl + d) % 4], wzb.at[d - 1], net.go(zl=d)) for d in (1, 2, 3)]
        yield
        total = wsm[zl].astype(F32)
        for d in range(3):
            sent[d].wait_recv()
            total += wzb[d].astype(F32)
        spot = 4 * x + zl
        wfin[spot] = total.astype(BF16)
        sent = [net.send(wfin.at[spot], wfin.at[spot], net.go(zl=d)) for d in (1, 2, 3)]
        yield
        for copy in sent:
            copy.wait_recv()
        rows = pl.ds(4 * x, 4)
        sent = [net.send(wfin.at[rows], wfin.at[rows], net.go(x=d)) for d in (1, 2, 3)]
        yield
        for copy in sent:
            copy.wait_recv()
        for k in range(8):
            cols = slice(k * HD, (k + 1) * HD)
            gw_ref[0:64, cols] = wfin[2 * k]
            gw_ref[64:128, cols] = wfin[2 * k + 1]

    small = small_sums()
    next(small)
    next(outward)
    for copy in sent:
        copy.wait_recv()
    sent = [net.send(gpg.at[every, y, c], gpg.at[every, y, c], net.go(y=d)) for d in (1, 2, 3)]
    next(outward)
    next(small)
    for copy in sent:
        copy.wait_recv()
    other = net.send(gpg.at[every, every, c], gpg.at[every, every, c], to_c)
    swap_qkv(2)
    next(outward)
    next(small)
    other.wait_recv()
    gpr[...] = gpg[...].reshape(32 * ROWS, HD).astype(F32)
    for k in range(8):
        gpn[:, k * HD : (k + 1) * HD] = gpr[pl.ds(k, L, stride=8), :].astype(BF16)
    back = nn(gpn[...], jnp.concatenate([mt[...].reshape(DD, HD), wit[...]], axis=1))
    ghs[...] = back[:, HD:].astype(BF16)

    grad_heads = back[:, :HD].astype(BF16)
    next(outward)
    probs = probs_s[...]
    grad_probs = nt(grad_heads, vs[...])
    inside = jnp.sum(probs * grad_probs, axis=-1, keepdims=True)
    grad_scores = (probs * (grad_probs - inside) * scale).astype(BF16)
    gr[0, 0] = nn(grad_scores, ks[...]).astype(BF16)
    gr[0, 1] = tn(grad_scores, qs[...]).astype(BF16)
    gr[0, 2] = tn(probs.astype(BF16), grad_heads).astype(BF16)
    grads_copy = net.send(gr.at[0], gr.at[1], to_c)
    next(outward)
    next(small)
    for copy in partner_qkv:
        copy.wait_recv()
    sums = weight_sums()
    grads_copy.wait_recv()

    def fill_in(yy, pair):
        left = jnp.concatenate([gr[i, j] for i in range(2) for j in range(3)], axis=1)
        right = []
        for zz in pair:
            right.append(
                jnp.concatenate(
                    [wq[j, zz, yy, c] for j in range(3)] + [wqp[j, zz, yy] for j in range(3)],
                    axis=1,
                )
            )
        term = nt(left, jnp.concatenate(right, axis=0)).astype(BF16)
        p3[pair[0], yy] = term[:, :HD]
        p3[pair[1], yy] = term[:, HD:]

    def keep_grad(summed):
        gx_ref[...] = (ghs[...].astype(F32) + summed).astype(BF16)

    for i, _ in enumerate(scatter_ring(net, p3, fill_in, bufs2, keep_grad)):
        if i == 1:
            next(outward, None)
        if i >= 1:
            next(sums, None)
        if i >= 2:
            next(small, None)
    for _ in small:
        pass
    for _ in sums:
        pass
    net.drain()


def ring_buffers():
    return [
        pltpu.VMEM((4, HALF, HD), BF16),
        pltpu.VMEM((4, HALF, HD), BF16),
        pltpu.VMEM((4, L, HD), BF16),
        pltpu.VMEM((4, L, HD), BF16),
        pltpu.VMEM((3, L, HD), BF16),
        pltpu.VMEM((HALF, HD), BF16),
        pltpu.VMEM((HALF, HD), BF16),
        pltpu.VMEM((L, HD), BF16),
        pltpu.VMEM((L, HD), BF16),
    ]


def shards(layer_input, frame_mask, w_qkv, w_out, w_in, step_embed, depth_gain, cotangent):
    def v(*shape, kind=BF16):
        return pltpu.VMEM(shape, kind)

    vmem = pl.BlockSpec(memory_space=pltpu.VMEM)
    hbm = pl.BlockSpec(memory_space=pltpu.HBM)
    scratch = [
        v(4, 4, 2, L, HD),
        v(1, L, kind=jnp.int32),
        v(STEPS, DD),
        v(DD),
        v(3, 4, 4, 2, HD, HD),
        v(3, 4, 4, HD, HD),
        v(HD, 32 * HD),
        v(16, HD, HD),
        v(HD, DD),
        v(DD, HD),
        v(DD, HD),
        v(STEPS, FR, DD),
        v(4, 4, 2, PIECE, HD),
        v(4, 4, PIECE, HD),
        v(4, 4, PIECE, HD),
        v(L, 3 * HD, kind=F32),
        v(L, HD),
        v(L, HD),
        v(L, HD),
        v(L, L, kind=F32),
        v(2, L, HD),
        v(4, 4, L, HD),
        v(L, HD),
        v(32 * ROWS, HD, kind=F32),
        v(4, 4, ROWS, HD),
        v(3, 4, ROWS, HD),
        v(4, ROWS, HD),
        v(3, ROWS, HD),
        v(ROWS, HD, kind=F32),
        v(ROWS, HD, kind=F32),
        v(4, 4, 2, ROWS, HD),
        v(32 * ROWS, HD, kind=F32),
        v(L, DD),
        v(L, HD),
        v(4, 4, L, HD),
        v(2, 3, L, HD),
        v(24, DD, kind=F32),
        v(16, 64, HD),
        v(3, 4, 64, HD),
        v(4, 64, HD),
        v(3, 64, HD),
        v(16, 64, HD),
        v(4, 4, 16, HD, kind=F32),
        v(3, 4, 16, HD, kind=F32),
        v(4, 16, HD, kind=F32),
        v(3, 16, HD, kind=F32),
        v(4, 16, HD, kind=F32),
        v(4, 16, HD, kind=F32),
        v(2, 16, HD, kind=F32),
        v(4, 4, 16, HD, kind=F32),
        *ring_buffers(),
        *ring_buffers(),
        pltpu.SemaphoreType.DMA((N_SEM,)),
        pltpu.SemaphoreType.DMA((N_SEM,)),
        pltpu.SemaphoreType.DMA((8,)),
    ]
    grad_x, grad_in, grad_step, grad_gain = pl.pallas_call(
        kernel,
        out_shape=(
            jax.ShapeDtypeStruct((L, HD), BF16),
            jax.ShapeDtypeStruct((HD, DD), BF16),
            jax.ShapeDtypeStruct((STEPS, DD), F32),
            jax.ShapeDtypeStruct((1, DD), F32),
        ),
        in_specs=[hbm] * 8,
        out_specs=(vmem,) * 4,
        scratch_shapes=scratch,
        compiler_params=pltpu.CompilerParams(
            collective_id=0, has_side_effects=True, vmem_limit_bytes=60 * 1024 * 1024
        ),
    )(
        layer_input[0],
        frame_mask,
        step_embed,
        depth_gain,
        w_qkv.reshape(3, 4, 4, 2, HD, HD),
        w_out,
        w_in,
        jnp.transpose(cotangent[0], (1, 0, 2)),
    )
    return (grad_x[None], grad_in, grad_step, grad_gain[0])


def solution(mesh):
    return jax.shard_map(
        shards,
        mesh=mesh,
        in_specs=(
            P("dp", None, "tensor"),
            P("dp", None),
            P(None, None, "tensor"),
            P("tensor", None),
            P("tensor", None),
            P(),
            P(),
            P("dp", "tensor", None, None),
        ),
        out_specs=(P("dp", None, "tensor"), P("tensor", None), P(), P()),
        check_vma=False,
    )
```

time: 1200 us -> 113 us (0.09)
  waiting for transfers between devices: 853 us -> 0 us
  blocking collectives: 239 us -> 0 us
  Pallas kernels: 0 us -> 106 us
  starting transfers between devices: 56 us -> 0 us
  matrix products: 15.1 us -> 0 us
  between operations: 15.1 us -> 0.64 us
  local copies, waits for them, and re-layouts: 18 us -> 5.9 us
    psum x2 -> x0, waiting for transfers between devices: 607 us -> none  [the longest x1 441 us: shards(): step_sum, gain_sum = lax.psum((grad_step, grad_gain), ('dp', 'tensor'))]
    all_gather x3 -> x0, waiting for transfers between devices: 238 us -> none  [the longest x1 91.5 us: shards(): lax.all_gather(layer_input, 'tensor', axis=2, tiled=True)[0]]
    psum x1 -> x0, blocking collectives: 107 us -> none  [shards(): step_sum, gain_sum = lax.psum((grad_step, grad_gain), ('dp', 'tensor'))]
    pallas_call x0 -> x1, Pallas kernels: none -> 106 us  [shards(): pl.pallas_call(kernel, out_shape=(jax.ShapeDtypeStruct((L, HD), BF16), ja...]
    unnamed x1 -> x0, blocking collectives: 81.6 us -> none
    all_gather x1 -> x0, blocking collectives: 50.8 us -> none  [shards(): all_grads = lax.all_gather(grad_proj, 'tensor', axis=0, tiled=True)]
    unnamed x9 -> x0, starting transfers between devices: 37.6 us -> none
    all_to_all x1 -> x0, starting transfers between devices: 18.2 us -> none  [shards(): lax.all_to_all(w_out, 'tensor', split_axis=1, concat_axis=0, tiled=True)]
  transfers between devices with their start and end apart: 15 -> 0, of which waited for: 6 -> 0; matrix products, arithmetic and copies ran while one was open for 1% -> 0% of each run, Pallas kernels for 0% -> 0%
where the time goes in v1:
time: 113 us; the launch traced here: 112 us
  Pallas kernels  106 us (94%)
  local copies, waits for them, and re-layouts  5.9 us (5%)
    pallas_call x1, Pallas kernels, shards(): pl.pallas_call(kernel, out_shape=(jax.ShapeDtypeStruct((L, HD), BF16), ja...  106 us
    unnamed x4, local copies, waits for them, and re-layouts  5.9 us

profile of v1, /device:TPU:24, one launch (start us, length us, event | category | flops | bytes accessed | tf_op | source)
XLA Modules:
  0.0 112.2 jit_solution(14970145940261415376)
XLA Ops:
  0.6 105.7 %shard_map.111 = (bf16[192,128]{1,0:T(8,128)(2,1)}, bf16[128,1024]{1,0:T(8,128)(2,1)}, f32[17,1024]{1,0:T(8,128)}, f32[1,1024]{1,0:T(1,128)}) custom-call(bf16[192,128]{1,0:T(8,128)(2,1)} %bitcast.9, s32[1,192]{1,0:T(1,128)} %mask_hbm.1, bf16[17,1024]{1,0:T(8,128)(2,1)} %step_hbm.1, bf16[1024]{0:T(1024)(128)(2,1)} %gain_hbm.1, ...), custom_call_target="tpu_custom_call" | custom-call | tf_op jit(solution)/shard_map/pallas_call | solution.py:684
  106.3 1.4 %copy.16 = bf16[1,192,128]{2,1,0:T(8,128)(2,1)} copy(bf16[1,192,128]{2,1,0:T(8,128)(2,1)} %bitcast.10) | data formatting | bytes 98304
  107.8 1.7 %copy.17 = bf16[128,1024]{1,0:T(8,128)(2,1)} copy(bf16[128,1024]{1,0:T(8,128)(2,1)} %get-tuple-element.17) | data formatting | bytes 524288
  109.4 1.5 %copy.18 = f32[17,1024]{1,0:T(8,128)} copy(f32[17,1024]{1,0:T(8,128)} %get-tuple-element.18) | data formatting | bytes 139264
  111.0 1.3 %copy.19 = f32[1024]{0:T(1024)} copy(f32[1024]{0:T(1024)} %bitcast.11) | data formatting | bytes 8192

commit v2 on v1

--- a/solution.py
+++ b/solution.py
@@ -126,7 +126,15 @@
 
     def spread(self, i):
         zz, y = self.planes[i], self.net.y
-        self.along[i] = (self.whole(zz, y, self.to_yp), self.whole(zz, y, self.to_ym))
+        if i == 3:
+            self.along[i] = (
+                self.part(zz, y, LO, self.to_yp),
+                self.part(zz, y, HI, self.to_ym),
+                self.part(zz, y, HI, self.to_yp),
+                self.part(zz, y, LO, self.to_ym),
+            )
+        else:
+            self.along[i] = (self.whole(zz, y, self.to_yp), self.whole(zz, y, self.to_ym))
         self.across[i] = []
         self.over(i, zz, y)
 
@@ -139,11 +147,13 @@
         yp, ym, _ = around(self.net.y)
         self.along[i][0].wait_recv()
         first = self.part(zz, ym, LO, self.to_yp)
-        self.over(i, zz, ym)
         self.along[i][1].wait_recv()
         second = self.part(zz, yp, HI, self.to_ym)
+        self.forward[i] = (first, second)
+        for copy in self.along[i][2:]:
+            copy.wait_recv()
+        self.over(i, zz, ym)
         self.over(i, zz, yp)
-        self.forward[i] = (first, second)
 
     def land(self, i):
         for copy in self.forward[i]:
@@ -158,53 +168,55 @@
             copy.wait_recv()
 
 
-def scatter_ring(net, p, fill, bufs, done, early=False):
+def scatter_ring(net, p, fill, bufs, done, ahead=False):
     ya, yb, yup, ydn, q, za, zb, zup, zdn = bufs
     z, y = net.z, net.y
     zp, zm, z2 = around(z)
     yp, ym, y2 = around(y)
     to_zp, to_zm, to_yp, to_ym = net.go(z=1), net.go(z=3), net.go(y=1), net.go(y=3)
     order = (z2, zp, zm, z)
-
     pairs = (order[:2], order[2:])
-    if early:
+
+    far, near = [], [[], [], [], []]
+    if ahead:
         for yy in (y2, yp, ym, y):
             for pair in pairs:
                 fill(yy, pair)
         yield
-    far = []
     for pair in pairs:
-        if not early:
+        if not ahead:
             fill(y2, pair)
         for zz in pair:
-            far.append(
-                (
-                    net.send(p.at[zz, y2, LO], ya.at[zz], to_yp),
-                    net.send(p.at[zz, y2, HI], yb.at[zz], to_ym),
-                )
-            )
-    yield
-    if not early:
-        for pair in pairs:
+            a = net.send(p.at[zz, y2, LO], ya.at[zz], to_yp)
+            far.append((a, net.send(p.at[zz, y2, HI], yb.at[zz], to_ym)))
+
+    def at_once(i):
+        zz = order[i]
+        near[i].append(net.send(p.at[zz, yp, HI], yup.at[zz, HI], to_yp))
+        near[i].append(net.send(p.at[zz, ym, LO], ydn.at[zz, LO], to_ym))
+
+    for j, pair in enumerate(pairs):
+        if not ahead:
             fill(yp, pair)
             fill(ym, pair)
-        yield
-    near = []
+        at_once(2 * j)
+        at_once(2 * j + 1)
+    yield
     for i, zz in enumerate(order):
         far[i][0].wait_recv()
         p[zz, yp, LO] = (p[zz, yp, LO].astype(F32) + ya[zz].astype(F32)).astype(BF16)
-        up = net.send(p.at[zz, yp], yup.at[zz], to_yp)
+        near[i].append(net.send(p.at[zz, yp, LO], yup.at[zz, LO], to_yp))
         far[i][1].wait_recv()
         p[zz, ym, HI] = (p[zz, ym, HI].astype(F32) + yb[zz].astype(F32)).astype(BF16)
-        near.append((up, net.send(p.at[zz, ym], ydn.at[zz], to_ym)))
-    if not early:
+        near[i].append(net.send(p.at[zz, ym, HI], ydn.at[zz, HI], to_ym))
+    if not ahead:
         for pair in pairs:
             fill(y, pair)
     yield
 
     def mine(i):
-        near[i][0].wait_recv()
-        near[i][1].wait_recv()
+        for copy in near[i]:
+            copy.wait_recv()
         zz = order[i]
         return p[zz, y].astype(F32) + yup[zz].astype(F32) + ydn[zz].astype(F32)
 
@@ -213,19 +225,21 @@
     b = net.send(q.at[0, HI], zb, to_zm)
     yield
     q[1] = mine(1).astype(BF16)
+    last = [net.send(q.at[1, HI], zup.at[HI], to_zp)]
     q[2] = mine(2).astype(BF16)
+    last.append(net.send(q.at[2, LO], zdn.at[LO], to_zm))
     yield
     a.wait_recv()
     q[1, LO] = (q[1, LO].astype(F32) + za[...].astype(F32)).astype(BF16)
-    up = net.send(q.at[1], zup, to_zp)
+    last.append(net.send(q.at[1, LO], zup.at[LO], to_zp))
     b.wait_recv()
     q[2, HI] = (q[2, HI].astype(F32) + zb[...].astype(F32)).astype(BF16)
-    down = net.send(q.at[2], zdn, to_zm)
+    last.append(net.send(q.at[2, HI], zdn.at[HI], to_zm))
     yield
     total = mine(3)
     yield
-    up.wait_recv()
-    down.wait_recv()
+    for copy in last:
+        copy.wait_recv()
     done(total + zup[...].astype(F32) + zdn[...].astype(F32))
 
 
@@ -316,9 +330,9 @@
         acc[...] = term if i == 0 else acc[...] + term
 
     product = weight_product()
-    next(product)
     gather = Gather(net, xg)
     gather.begin()
+    next(product)
     next(product)
     gather.along_z()
     next(product)
@@ -378,8 +392,9 @@
     hp[0] = nn(probs.astype(BF16), value).astype(BF16)
     heads_copy = net.send(hp.at[0], hp.at[1], to_c)
     partner_in.wait_recv()
+    heads_copy.wait_recv()
+
     next(product, None)
-    heads_copy.wait_recv()
 
     left = jnp.concatenate([hp[0], hp[1], xg[z, y, c], xg[z, y, 1 - c]], axis=1)
     right = jnp.concatenate(
@@ -393,6 +408,7 @@
             rows = pl.ds(pl.multiple_of((8 * i + 2 * j + c) * ROWS, 8), ROWS)
             p2[j, i] = pf[rows, :].astype(BF16)
     sent = [net.send(p2.at[(y + d) % 4], pyb.at[d - 1], net.go(y=d)) for d in (1, 2, 3)]
+
     def fill_out(yy, pair):
         left = jnp.concatenate([hp[0], hp[1]], axis=1)
         right = []
@@ -406,7 +422,7 @@
     def keep_hidden(summed):
         hid[...] = (xg[z, y, c].astype(F32) + summed).astype(BF16)
 
-    outward = scatter_ring(net, p1, fill_out, bufs1, keep_hidden, early=True)
+    outward = scatter_ring(net, p1, fill_out, bufs1, keep_hidden, ahead=True)
     partner_out.wait_recv()
     next(outward)
     total = p2[y].astype(F32)
@@ -445,6 +461,7 @@
     gpg[z, y, c] = gpf[...].astype(BF16)
 
     sent = [net.send(gpg.at[z, y, c], gpg.at[z, y, c], net.go(z=d)) for d in (1, 2, 3)]
+    next(outward)
     rows_s[STEPS : STEPS + 1, :] = jnp.sum(gain_rows, axis=0, keepdims=True)
     for k in range(8):
         cols = slice(k * HD, (k + 1) * HD)
@@ -535,29 +552,27 @@
             gw_ref[0:64, cols] = wfin[2 * k]
             gw_ref[64:128, cols] = wfin[2 * k + 1]
 
-    small = small_sums()
-    next(small)
-    next(outward)
     for copy in sent:
         copy.wait_recv()
     sent = [net.send(gpg.at[every, y, c], gpg.at[every, y, c], net.go(y=d)) for d in (1, 2, 3)]
     next(outward)
-    next(small)
     for copy in sent:
         copy.wait_recv()
     other = net.send(gpg.at[every, every, c], gpg.at[every, every, c], to_c)
     swap_qkv(2)
+    small = small_sums()
+    next(small)
     next(outward)
-    next(small)
     other.wait_recv()
     gpr[...] = gpg[...].reshape(32 * ROWS, HD).astype(F32)
     for k in range(8):
         gpn[:, k * HD : (k + 1) * HD] = gpr[pl.ds(k, L, stride=8), :].astype(BF16)
     back = nn(gpn[...], jnp.concatenate([mt[...].reshape(DD, HD), wit[...]], axis=1))
     ghs[...] = back[:, HD:].astype(BF16)
+    next(outward)
+    next(small)
 
     grad_heads = back[:, :HD].astype(BF16)
-    next(outward)
     probs = probs_s[...]
     grad_probs = nt(grad_heads, vs[...])
     inside = jnp.sum(probs * grad_probs, axis=-1, keepdims=True)
@@ -568,9 +583,9 @@
     grads_copy = net.send(gr.at[0], gr.at[1], to_c)
     next(outward)
     next(small)
+    sums = weight_sums()
     for copy in partner_qkv:
         copy.wait_recv()
-    sums = weight_sums()
     grads_copy.wait_recv()
 
     def fill_in(yy, pair):
@@ -591,17 +606,25 @@
         gx_ref[...] = (ghs[...].astype(F32) + summed).astype(BF16)
 
     for i, _ in enumerate(scatter_ring(net, p3, fill_in, bufs2, keep_grad)):
-        if i == 1:
+        if i == 0:
             next(outward, None)
-        if i >= 1:
-            next(sums, None)
-        if i >= 2:
-            next(small, None)
+        if i < 4:
+            next(sums)
+        next(small, None)
     for _ in small:
         pass
     for _ in sums:
         pass
     net.drain()
+
+
+def hand_out(*refs):
+    sems = refs[8]
+    copies = [pltpu.make_async_copy(refs[i], refs[4 + i], sems.at[i]) for i in range(4)]
+    for copy in copies:
+        copy.start()
+    for copy in copies:
+        copy.wait()
 
 
 def ring_buffers():
@@ -684,10 +707,10 @@
     grad_x, grad_in, grad_step, grad_gain = pl.pallas_call(
         kernel,
         out_shape=(
-            jax.ShapeDtypeStruct((L, HD), BF16),
-            jax.ShapeDtypeStruct((HD, DD), BF16),
-            jax.ShapeDtypeStruct((STEPS, DD), F32),
-            jax.ShapeDtypeStruct((1, DD), F32),
+            pltpu.VMEM((L, HD), BF16),
+            pltpu.VMEM((HD, DD), BF16),
+            pltpu.VMEM((STEPS, DD), F32),
+            pltpu.VMEM((1, DD), F32),
         ),
         in_specs=[hbm] * 8,
         out_specs=(vmem,) * 4,
@@ -705,6 +728,19 @@
         w_in,
         jnp.transpose(cotangent[0], (1, 0, 2)),
     )
+    grad_x, grad_in, grad_step, grad_gain = pl.pallas_call(
+        hand_out,
+        out_shape=(
+            jax.ShapeDtypeStruct((L, HD), BF16),
+            jax.ShapeDtypeStruct((HD, DD), BF16),
+            jax.ShapeDtypeStruct((STEPS, DD), F32),
+            jax.ShapeDtypeStruct((1, DD), F32),
+        ),
+        in_specs=[vmem] * 4,
+        out_specs=(hbm,) * 4,
+        scratch_shapes=[pltpu.SemaphoreType.DMA((4,))],
+        compiler_params=pltpu.CompilerParams(vmem_limit_bytes=2 * 1024 * 1024),
+    )(grad_x, grad_in, grad_step, grad_gain)
     return (grad_x[None], grad_in, grad_step, grad_gain[0])
 
 

time: 113 us -> 106 us (0.938)
  local copies, waits for them, and re-layouts: 5.9 us -> 0 us
    unnamed x4 -> x0, local copies, waits for them, and re-layouts: 5.9 us -> none
    pallas_call x1 -> x2, Pallas kernels: 106 us -> 105 us  [the longest x1 104 us: shards(): pl.pallas_call(kernel, out_shape=(pltpu.VMEM((L, HD), BF16), pltpu.VMEM((...]
where the time goes in v2:
time: 106 us; the launch traced here: 105 us
  Pallas kernels  105 us (99%)
    pallas_call x1, Pallas kernels, shards(): pl.pallas_call(kernel, out_shape=(pltpu.VMEM((L, HD), BF16), pltpu.VMEM((...  104 us

profile of v2, /device:TPU:24, one launch (start us, length us, event | category | flops | bytes accessed | tf_op | source)
XLA Modules:
  0.0 105.3 jit_solution(10169748486130467676)
XLA Ops:
  0.6 103.8 %shard_map.111 = (bf16[192,128]{1,0:T(8,128)(2,1)S(1)}, bf16[128,1024]{1,0:T(8,128)(2,1)S(1)}, f32[17,1024]{1,0:T(8,128)S(1)}, f32[1,1024]{1,0:T(1,128)S(1)}) custom-call(bf16[192,128]{1,0:T(8,128)(2,1)} %bitcast.9, s32[1,192]{1,0:T(1,128)} %mask_hbm.1, bf16[17,1024]{1,0:T(8,128)(2,1)} %step_hbm.1, bf16[1024]{0:T(1024)(128)(2,1)} %gain_hbm.1, ...), custom_call_target="tpu_custom_call" | custom-call | tf_op jit(solution)/shard_map/pallas_call | solution.py:707
  104.5 0.8 shard_map.112

commit v3 on v2

--- a/solution.py
+++ b/solution.py
@@ -447,6 +447,8 @@
     grad_rows = jnp.zeros((FR, DD), F32)
     gain_rows = jnp.zeros((FR, DD), F32)
     for s in range(STEPS):
+        if s == 8:
+            next(outward)
         inner = proj + stepv[s : s + 1, :].astype(F32)
         inverse = lax.rsqrt(jnp.mean(inner * inner, axis=-1, keepdims=True) + 1e-06)
         arriving = cot[s].astype(F32)
@@ -556,6 +558,7 @@
         copy.wait_recv()
     sent = [net.send(gpg.at[every, y, c], gpg.at[every, y, c], net.go(y=d)) for d in (1, 2, 3)]
     next(outward)
+    next(outward)
     for copy in sent:
         copy.wait_recv()
     other = net.send(gpg.at[every, every, c], gpg.at[every, every, c], to_c)
@@ -563,13 +566,15 @@
     small = small_sums()
     next(small)
     next(outward)
+    next(outward, None)
     other.wait_recv()
     gpr[...] = gpg[...].reshape(32 * ROWS, HD).astype(F32)
     for k in range(8):
         gpn[:, k * HD : (k + 1) * HD] = gpr[pl.ds(k, L, stride=8), :].astype(BF16)
     back = nn(gpn[...], jnp.concatenate([mt[...].reshape(DD, HD), wit[...]], axis=1))
     ghs[...] = back[:, HD:].astype(BF16)
-    next(outward)
+    sums = weight_sums()
+    next(sums)
     next(small)
 
     grad_heads = back[:, :HD].astype(BF16)
@@ -581,9 +586,8 @@
     gr[0, 1] = tn(grad_scores, qs[...]).astype(BF16)
     gr[0, 2] = tn(probs.astype(BF16), grad_heads).astype(BF16)
     grads_copy = net.send(gr.at[0], gr.at[1], to_c)
-    next(outward)
+    next(sums)
     next(small)
-    sums = weight_sums()
     for copy in partner_qkv:
         copy.wait_recv()
     grads_copy.wait_recv()
@@ -606,9 +610,7 @@
         gx_ref[...] = (ghs[...].astype(F32) + summed).astype(BF16)
 
     for i, _ in enumerate(scatter_ring(net, p3, fill_in, bufs2, keep_grad)):
-        if i == 0:
-            next(outward, None)
-        if i < 4:
+        if i < 2:
             next(sums)
         next(small, None)
     for _ in small:

time: 106 us -> 109 us (1.028)
  Pallas kernels: 105 us -> 108 us
    pallas_call x1, Pallas kernels: 104 us -> 108 us  [shards(): pl.pallas_call(kernel, out_shape=(pltpu.VMEM((L, HD), BF16), pltpu.VMEM((...]
where the time goes in v3:
time: 109 us
  Pallas kernels  108 us (99%)
    pallas_call x1, Pallas kernels, shards(): pl.pallas_call(kernel, out_shape=(pltpu.VMEM((L, HD), BF16), pltpu.VMEM((...  108 us

profile of v3, /device:TPU:24, one launch (start us, length us, event | category | flops | bytes accessed | tf_op | source)
XLA Modules:
  0.0 108.9 jit_solution(14208527141713487872)
XLA Ops:
  0.6 107.5 %shard_map.111 = (bf16[192,128]{1,0:T(8,128)(2,1)S(1)}, bf16[128,1024]{1,0:T(8,128)(2,1)S(1)}, f32[17,1024]{1,0:T(8,128)S(1)}, f32[1,1024]{1,0:T(1,128)S(1)}) custom-call(bf16[192,128]{1,0:T(8,128)(2,1)} %bitcast.9, s32[1,192]{1,0:T(1,128)} %mask_hbm.1, bf16[17,1024]{1,0:T(8,128)(2,1)} %step_hbm.1, bf16[1024]{0:T(1024)(128)(2,1)} %gain_hbm.1, ...), custom_call_target="tpu_custom_call" | custom-call | tf_op jit(solution)/shard_map/pallas_call | solution.py:709
  108.1 0.8 shard_map.112

commit v4 on v2

--- a/solution.py
+++ b/solution.py
@@ -105,7 +105,8 @@
         self.dn_hi = self.part(z, y, HI, to_zm)
         self.up_hi = self.part(z, y, HI, to_zp)
         self.dn_lo = self.part(z, y, LO, to_zm)
-        self.spread(0)
+        self.spread(0, LO)
+        self.spread(0, HI)
 
     def along_z(self):
         y = self.net.y
@@ -114,29 +115,26 @@
         self.on = self.part(self.planes[1], y, LO, to_zp)
         self.dn_hi.wait_recv()
         self.back = self.part(self.planes[2], y, HI, to_zm)
+        self.spread(1, LO)
+        self.spread(2, HI)
         self.up_hi.wait_recv()
-        self.spread(1)
+        self.spread(1, HI)
         self.dn_lo.wait_recv()
-        self.spread(2)
+        self.spread(2, LO)
 
     def far_z(self):
         self.on.wait_recv()
+        self.spread(3, LO)
         self.back.wait_recv()
-        self.spread(3)
-
-    def spread(self, i):
+        self.spread(3, HI)
+
+    def spread(self, i, rows):
         zz, y = self.planes[i], self.net.y
-        if i == 3:
-            self.along[i] = (
-                self.part(zz, y, LO, self.to_yp),
-                self.part(zz, y, HI, self.to_ym),
-                self.part(zz, y, HI, self.to_yp),
-                self.part(zz, y, LO, self.to_ym),
-            )
-        else:
-            self.along[i] = (self.whole(zz, y, self.to_yp), self.whole(zz, y, self.to_ym))
-        self.across[i] = []
-        self.over(i, zz, y)
+        up = self.part(zz, y, rows, self.to_yp)
+        self.along[i, rows.start] = (up, self.part(zz, y, rows, self.to_ym))
+        self.across.setdefault(i, [])
+        if rows.start == (HI if i == 3 else LO).start:
+            self.over(i, zz, y)
 
     def over(self, i, zz, yy):
         if i == 3:
@@ -145,14 +143,15 @@
     def turn(self, i):
         zz = self.planes[i]
         yp, ym, _ = around(self.net.y)
-        self.along[i][0].wait_recv()
+        lo, hi = self.along[i, LO.start], self.along[i, HI.start]
+        lo[0].wait_recv()
         first = self.part(zz, ym, LO, self.to_yp)
-        self.along[i][1].wait_recv()
+        hi[1].wait_recv()
         second = self.part(zz, yp, HI, self.to_ym)
         self.forward[i] = (first, second)
-        for copy in self.along[i][2:]:
-            copy.wait_recv()
+        hi[0].wait_recv()
         self.over(i, zz, ym)
+        lo[1].wait_recv()
         self.over(i, zz, yp)
 
     def land(self, i):
@@ -333,7 +332,6 @@
     gather = Gather(net, xg)
     gather.begin()
     next(product)
-    next(product)
     gather.along_z()
     next(product)
     gather.turn(0)
@@ -345,6 +343,7 @@
     gather.turn(3)
     gather.land(1)
     gather.land(2)
+    next(product)
     loads["w_qkv"].wait()
     plane(0)
     next(product)
@@ -385,12 +384,12 @@
     col = lax.broadcasted_iota(jnp.int32, (L, L), 1)
     allowed = (col <= row) & ((maskv[...] == 1) | (col == row))
     scores = jnp.where(allowed, nt(query, key_rows) * scale, -1e30)
-    next(product)
     raised = jnp.exp(scores - jnp.max(scores, axis=-1, keepdims=True))
     probs = raised / jnp.sum(raised, axis=-1, keepdims=True)
     probs_s[...] = probs
     hp[0] = nn(probs.astype(BF16), value).astype(BF16)
     heads_copy = net.send(hp.at[0], hp.at[1], to_c)
+    next(product)
     partner_in.wait_recv()
     heads_copy.wait_recv()
 
@@ -570,7 +569,6 @@
     back = nn(gpn[...], jnp.concatenate([mt[...].reshape(DD, HD), wit[...]], axis=1))
     ghs[...] = back[:, HD:].astype(BF16)
     next(outward)
-    next(small)
 
     grad_heads = back[:, :HD].astype(BF16)
     probs = probs_s[...]

time: 106 us -> 107 us (level)
  no operation moved by 1% of the time
where the time goes in v4:
time: 107 us; the launch traced here: 105 us
  Pallas kernels  105 us (98%)
    pallas_call x1, Pallas kernels, shards(): pl.pallas_call(kernel, out_shape=(pltpu.VMEM((L, HD), BF16), pltpu.VMEM((...  104 us

profile of v4, /device:TPU:24, one launch (start us, length us, event | category | flops | bytes accessed | tf_op | source)
XLA Modules:
  0.0 105.3 jit_solution(448175153236821498)
XLA Ops:
  0.6 103.9 %shard_map.111 = (bf16[192,128]{1,0:T(8,128)(2,1)S(1)}, bf16[128,1024]{1,0:T(8,128)(2,1)S(1)}, f32[17,1024]{1,0:T(8,128)S(1)}, f32[1,1024]{1,0:T(1,128)S(1)}) custom-call(bf16[192,128]{1,0:T(8,128)(2,1)} %bitcast.9, s32[1,192]{1,0:T(1,128)} %mask_hbm.1, bf16[17,1024]{1,0:T(8,128)(2,1)} %step_hbm.1, bf16[1024]{0:T(1024)(128)(2,1)} %gain_hbm.1, ...), custom_call_target="tpu_custom_call" | custom-call | tf_op jit(solution)/shard_map/pallas_call | solution.py:705
  104.5 0.8 shard_map.112

commit v5 on v2

--- a/solution.py
+++ b/solution.py
@@ -331,8 +331,23 @@
 
     product = weight_product()
     gather = Gather(net, xg)
+    next(product)
     gather.begin()
-    next(product)
+    partner_in = net.send(wit, witp, to_c)
+    spot = net.count
+    partner_out = net.make(wop, wop, to_c)
+    for i in range(16):
+        cols = pl.ds(pl.multiple_of((2 * i + 1 - c) * HD, HD), HD)
+        pltpu.make_async_remote_copy(
+            src_ref=wout_hbm.at[:, cols],
+            dst_ref=wop.at[i],
+            send_sem=send_sems.at[spot],
+            recv_sem=recv_sems.at[spot],
+            device_id=to_c,
+            device_id_type=MESH,
+        ).start()
+    net.open.append(partner_out)
+
     next(product)
     gather.along_z()
     next(product)
@@ -350,29 +365,13 @@
     next(product)
     plane(1)
     gather.land(3)
-    partner_in = net.send(wit, witp, to_c)
     plane(2)
     plane(3)
 
-    spot = net.count
-    partner_out = net.make(wop, wop, to_c)
-    for i in range(16):
-        cols = pl.ds(pl.multiple_of((2 * i + 1 - c) * HD, HD), HD)
-        pltpu.make_async_remote_copy(
-            src_ref=wout_hbm.at[:, cols],
-            dst_ref=wop.at[i],
-            send_sem=send_sems.at[spot],
-            recv_sem=recv_sems.at[spot],
-            device_id=to_c,
-            device_id_type=MESH,
-        ).start()
-    net.open.append(partner_out)
     partner_qkv = []
 
     def swap_qkv(j):
         partner_qkv.append(net.send(wqkv_hbm.at[j, every, every, 1 - c], wqp.at[j], to_c))
-
-    swap_qkv(0)
 
     query = acc[:, :HD].astype(BF16)
     key_rows = acc[:, HD : 2 * HD].astype(BF16)
@@ -408,6 +407,7 @@
             rows = pl.ds(pl.multiple_of((8 * i + 2 * j + c) * ROWS, 8), ROWS)
             p2[j, i] = pf[rows, :].astype(BF16)
     sent = [net.send(p2.at[(y + d) % 4], pyb.at[d - 1], net.go(y=d)) for d in (1, 2, 3)]
+    swap_qkv(0)
 
     def fill_out(yy, pair):
         left = jnp.concatenate([hp[0], hp[1]], axis=1)
@@ -431,6 +431,7 @@
         total += pyb[d].astype(F32)
     pq[...] = total.astype(BF16)
     sent = [net.send(pq.at[(z + d) % 4], pzb.at[d - 1], net.go(z=d)) for d in (1, 2, 3)]
+    swap_qkv(1)
 
     next(outward)
     total = pq[z].astype(F32)
@@ -438,7 +439,7 @@
         sent[d].wait_recv()
         total += pzb[d].astype(F32)
     pr[...] = total
-    swap_qkv(1)
+    swap_qkv(2)
 
     for name in ("step", "gain", "cot"):
         loads[name].wait()
@@ -559,7 +560,6 @@
     for copy in sent:
         copy.wait_recv()
     other = net.send(gpg.at[every, every, c], gpg.at[every, every, c], to_c)
-    swap_qkv(2)
     small = small_sums()
     next(small)
     next(outward)
@@ -570,7 +570,6 @@
     back = nn(gpn[...], jnp.concatenate([mt[...].reshape(DD, HD), wit[...]], axis=1))
     ghs[...] = back[:, HD:].astype(BF16)
     next(outward)
-    next(small)
 
     grad_heads = back[:, :HD].astype(BF16)
     probs = probs_s[...]

time: 106 us -> 107 us (level)
  no operation moved by 1% of the time
where the time goes in v5:
time: 107 us; the launch traced here: 106 us
  Pallas kernels  105 us (98%)
    pallas_call x1, Pallas kernels, shards(): pl.pallas_call(kernel, out_shape=(pltpu.VMEM((L, HD), BF16), pltpu.VMEM((...  104 us

profile of v5, /device:TPU:24, one launch (start us, length us, event | category | flops | bytes accessed | tf_op | source)
XLA Modules:
  0.0 105.9 jit_solution(15892350513676016982)
XLA Ops:
  0.6 104.5 %shard_map.111 = (bf16[192,128]{1,0:T(8,128)(2,1)S(1)}, bf16[128,1024]{1,0:T(8,128)(2,1)S(1)}, f32[17,1024]{1,0:T(8,128)S(1)}, f32[1,1024]{1,0:T(1,128)S(1)}) custom-call(bf16[192,128]{1,0:T(8,128)(2,1)} %bitcast.9, s32[1,192]{1,0:T(1,128)} %mask_hbm.1, bf16[17,1024]{1,0:T(8,128)(2,1)} %step_hbm.1, bf16[1024]{0:T(1024)(128)(2,1)} %gain_hbm.1, ...), custom_call_target="tpu_custom_call" | custom-call | tf_op jit(solution)/shard_map/pallas_call | solution.py:706
  105.1 0.8 shard_map.112

commit v6 on v5

--- a/solution.py
+++ b/solution.py
@@ -77,10 +77,11 @@
         self.open.append(copy)
         return copy
 
-    def drain(self):
-        for copy in self.open:
+    def drain(self, keep=0):
+        done = self.open[: len(self.open) - keep]
+        for copy in done:
             copy.wait_send()
-        self.open = []
+        self.open = self.open[len(done) :]
 
 
 class Gather:
@@ -175,32 +176,33 @@
     yp, ym, y2 = around(y)
     to_zp, to_zm, to_yp, to_ym = net.go(z=1), net.go(z=3), net.go(y=1), net.go(y=3)
     order = (z2, zp, zm, z)
-    pairs = (order[:2], order[2:])
+
+    def fill_rows(first, step, count):
+        @pl.loop(0, 2 * count)
+        def _(k):
+            j = k % 2
+            yy = (y + first + step * (k // 2)) % 4
+            fill(yy, ((z + 2 + j) % 4, (z + 5 - j) % 4))
 
     far, near = [], [[], [], [], []]
     if ahead:
-        for yy in (y2, yp, ym, y):
-            for pair in pairs:
-                fill(yy, pair)
-        yield
-    for pair in pairs:
-        if not ahead:
-            fill(y2, pair)
-        for zz in pair:
-            a = net.send(p.at[zz, y2, LO], ya.at[zz], to_yp)
-            far.append((a, net.send(p.at[zz, y2, HI], yb.at[zz], to_ym)))
+        fill_rows(0, 1, 4)
+        yield
+    else:
+        fill_rows(2, 0, 1)
+    for zz in order:
+        a = net.send(p.at[zz, y2, LO], ya.at[zz], to_yp)
+        far.append((a, net.send(p.at[zz, y2, HI], yb.at[zz], to_ym)))
 
     def at_once(i):
         zz = order[i]
         near[i].append(net.send(p.at[zz, yp, HI], yup.at[zz, HI], to_yp))
         near[i].append(net.send(p.at[zz, ym, LO], ydn.at[zz, LO], to_ym))
 
-    for j, pair in enumerate(pairs):
-        if not ahead:
-            fill(yp, pair)
-            fill(ym, pair)
-        at_once(2 * j)
-        at_once(2 * j + 1)
+    if not ahead:
+        fill_rows(1, 2, 2)
+    for i in range(4):
+        at_once(i)
     yield
     for i, zz in enumerate(order):
         far[i][0].wait_recv()
@@ -210,8 +212,7 @@
         p[zz, ym, HI] = (p[zz, ym, HI].astype(F32) + yb[zz].astype(F32)).astype(BF16)
         near[i].append(net.send(p.at[zz, ym, HI], ydn.at[zz, HI], to_ym))
     if not ahead:
-        for pair in pairs:
-            fill(y, pair)
+        fill_rows(0, 0, 1)
     yield
 
     def mine(i):
@@ -432,6 +433,7 @@
     pq[...] = total.astype(BF16)
     sent = [net.send(pq.at[(z + d) % 4], pzb.at[d - 1], net.go(z=d)) for d in (1, 2, 3)]
     swap_qkv(1)
+    net.drain(8)
 
     next(outward)
     total = pq[z].astype(F32)
@@ -463,6 +465,7 @@
 
     sent = [net.send(gpg.at[z, y, c], gpg.at[z, y, c], net.go(z=d)) for d in (1, 2, 3)]
     next(outward)
+    net.drain(20)
     rows_s[STEPS : STEPS + 1, :] = jnp.sum(gain_rows, axis=0, keepdims=True)
     for k in range(8):
         cols = slice(k * HD, (k + 1) * HD)
@@ -557,12 +560,14 @@
         copy.wait_recv()
     sent = [net.send(gpg.at[every, y, c], gpg.at[every, y, c], net.go(y=d)) for d in (1, 2, 3)]
     next(outward)
+    net.drain(16)
     for copy in sent:
         copy.wait_recv()
     other = net.send(gpg.at[every, every, c], gpg.at[every, every, c], to_c)
     small = small_sums()
     next(small)
     next(outward)
+    net.drain(12)
     other.wait_recv()
     gpr[...] = gpg[...].reshape(32 * ROWS, HD).astype(F32)
     for k in range(8):
@@ -610,6 +615,7 @@
         if i < 4:
             next(sums)
         next(small, None)
+        net.drain(24)
     for _ in small:
         pass
     for _ in sums:

time: 107 us -> 107 us (level)
  no operation moved by 1% of the time
where the time goes in v6:
time: 107 us; the launch traced here: 106 us
  Pallas kernels  105 us (98%)
    pallas_call x1, Pallas kernels, shards(): pl.pallas_call(kernel, out_shape=(pltpu.VMEM((L, HD), BF16), pltpu.VMEM((...  105 us

profile of v6, /device:TPU:24, one launch (start us, length us, event | category | flops | bytes accessed | tf_op | source)
XLA Modules:
  0.0 106.0 jit_solution(10155642056636568448)
XLA Ops:
  0.6 104.5 %shard_map.111 = (bf16[192,128]{1,0:T(8,128)(2,1)S(1)}, bf16[128,1024]{1,0:T(8,128)(2,1)S(1)}, f32[17,1024]{1,0:T(8,128)S(1)}, f32[1,1024]{1,0:T(1,128)S(1)}) custom-call(bf16[192,128]{1,0:T(8,128)(2,1)} %bitcast.9, s32[1,192]{1,0:T(1,128)} %mask_hbm.1, bf16[17,1024]{1,0:T(8,128)(2,1)} %step_hbm.1, bf16[1024]{0:T(1024)(128)(2,1)} %gain_hbm.1, ...), custom_call_target="tpu_custom_call" | custom-call | tf_op jit(solution)/shard_map/pallas_call | solution.py:712
  105.2 0.8 shard_map.112

commit v7 on v6

--- a/solution.py
+++ b/solution.py
@@ -587,7 +587,9 @@
     grads_copy = net.send(gr.at[0], gr.at[1], to_c)
     next(outward)
     next(small)
+    next(outward, None)
     sums = weight_sums()
+    next(sums)
     for copy in partner_qkv:
         copy.wait_recv()
     grads_copy.wait_recv()
@@ -610,9 +612,7 @@
         gx_ref[...] = (ghs[...].astype(F32) + summed).astype(BF16)
 
     for i, _ in enumerate(scatter_ring(net, p3, fill_in, bufs2, keep_grad)):
-        if i == 0:
-            next(outward, None)
-        if i < 4:
+        if 1 <= i < 4:
             next(sums)
         next(small, None)
         net.drain(24)

time: 107 us -> 107 us (level)
  no operation moved by 1% of the time
where the time goes in v7:
time: 107 us; the launch traced here: 106 us
  Pallas kernels  105 us (98%)
    pallas_call x1, Pallas kernels, shards(): pl.pallas_call(kernel, out_shape=(pltpu.VMEM((L, HD), BF16), pltpu.VMEM((...  105 us

profile of v7, /device:TPU:24, one launch (start us, length us, event | category | flops | bytes accessed | tf_op | source)
XLA Modules:
  0.0 106.0 jit_solution(14417875352110123634)
XLA Ops:
  0.6 104.6 %shard_map.111 = (bf16[192,128]{1,0:T(8,128)(2,1)S(1)}, bf16[128,1024]{1,0:T(8,128)(2,1)S(1)}, f32[17,1024]{1,0:T(8,128)S(1)}, f32[1,1024]{1,0:T(1,128)S(1)}) custom-call(bf16[192,128]{1,0:T(8,128)(2,1)} %bitcast.9, s32[1,192]{1,0:T(1,128)} %mask_hbm.1, bf16[17,1024]{1,0:T(8,128)(2,1)} %step_hbm.1, bf16[1024]{0:T(1024)(128)(2,1)} %gain_hbm.1, ...), custom_call_target="tpu_custom_call" | custom-call | tf_op jit(solution)/shard_map/pallas_call | solution.py:712
  105.2 0.8 shard_map.112
